TPU v7x, 32 devices: a whole 2x2x4 slice. The times are simulated.
32 devices in a mesh: grp: 2 (over y), lon: 4 (over x, core), lat: 4 (over z).
Axes of the slice: x: 2, y: 2, z: 4, core: 2. Of those that a mesh axis runs over, the one named last changes fastest.
Arguments:
- grid_field: bfloat16 [192, 1440, 256], P(('grp', 'lat'), 'lon'), parts along dimension 0, may hold values from -6 to 6
- weights: bfloat16 [512, 2, 256, 256], P(('lon', 'lat')), may hold values from -0.25 to 0.25
Outputs:
- upsampled: bfloat16 [192, 2880, 256], P(('grp', 'lat'), 'lon'), parts along dimension 0
There are 2 independent parts, one for each index of `grp`. A program takes and returns all parts, laid end to end along the dimension named above; an argument that names none is the same for every part. Nothing has to cross between parts.
All inputs are finite; a program needn't handle non-finite values.
Results may differ from a plain program's by a relative error of at most 0.014.
Values may be sent and summed in bfloat16 or wider, within the bound.
A program may use at most 320 MiB of HBM per device.

v0:
```python
import math
import jax
import jax.numpy as jnp
from jax import lax
from jax.sharding import PartitionSpec as P

NLON = 1440
M = 512


def analysis_table(lon_index):
    mode_index = jnp.arange(M, dtype=jnp.int32)
    norm_scale = 1.0 / math.sqrt(NLON)
    phase_index = mode_index[:, None] * lon_index[None, :] % NLON
    angles = 2.0 * math.pi / NLON * phase_index.astype(jnp.float32)
    table = jnp.stack([jnp.cos(angles) * norm_scale, -jnp.sin(angles) * norm_scale], 1)
    return table.reshape(2 * M, lon_index.shape[0]).astype(jnp.bfloat16)


def synthesis_table(out_index):
    mode_index = jnp.arange(M, dtype=jnp.int32)
    norm_scale = 1.0 / math.sqrt(NLON)
    phase_out = mode_index[:, None] * out_index[None, :] % (2 * NLON)
    angles_out = 2.0 * math.pi / (2 * NLON) * phase_out.astype(jnp.float32)
    factor = jnp.where(mode_index == 0, 1.0, 2.0).astype(jnp.float32)[:, None] * norm_scale
    table = jnp.stack([jnp.cos(angles_out) * factor, -jnp.sin(angles_out) * factor], 1)
    return table.reshape(2 * M, out_index.shape[0]).astype(jnp.bfloat16)


def mix_modes(slab_modes, portion):
    re_part = portion[:, 0]
    im_part = portion[:, 1]
    wide_weight = jnp.stack(
        [jnp.concatenate([re_part, im_part], -1), jnp.concatenate([-im_part, re_part], -1)], 1
    )
    return jnp.einsum(
        "mplc,mpcd->mld", slab_modes, wide_weight, preferred_element_type=jnp.float32
    ).astype(jnp.bfloat16)


def on_device(grid_field, weights):
    lat_rows, lon_dev, channels = grid_field.shape
    lon_count = lax.axis_size("lon")
    lon_rank = lax.axis_index("lon")
    modes_dev = M // lon_count
    lon_index = lon_rank * lon_dev + jnp.arange(lon_dev, dtype=jnp.int32)
    fwd_local = analysis_table(lon_index)
    table_rows = fwd_local
    summed = lax.psum_scatter(
        jnp.einsum(
            "kn,lnc->klc", table_rows, grid_field, preferred_element_type=jnp.float32
        ).astype(jnp.bfloat16),
        "lon",
        scatter_dimension=0,
        tiled=True,
    )
    lat_count = lax.axis_size("lat")
    own_modes = modes_dev // lat_count
    moved = lax.all_to_all(
        summed.reshape(lat_count, 2 * own_modes, lat_rows, channels), "lat", 0, 0, tiled=True
    )
    spectrum = (
        moved.reshape(lat_count, own_modes, 2, lat_rows, channels)
        .transpose(1, 2, 0, 3, 4)
        .reshape(own_modes, 2, lat_count * lat_rows, channels)
    )
    mixed_own = mix_modes(spectrum, weights)
    back = mixed_own.reshape(own_modes, lat_count, lat_rows, 2 * channels).transpose(1, 0, 2, 3)
    mixed_spec = lax.all_to_all(back, "lat", 0, 0, tiled=True).reshape(
        modes_dev, lat_rows, 2 * channels
    )
    out_dev = 2 * NLON // lon_count
    out_index = lon_rank * out_dev + jnp.arange(out_dev, dtype=jnp.int32)
    inv_local = synthesis_table(out_index).reshape(M, 2, out_dev)
    portion = lax.all_gather(mixed_spec, "lon", axis=0, tiled=True)
    count = portion.shape[0]
    table_rows = inv_local
    parted = portion.reshape(count, lat_rows, 2, channels)
    running = jnp.einsum("mlpc,mpn->lnc", parted, table_rows, preferred_element_type=jnp.float32)
    return running.astype(jnp.bfloat16)


def solution(mesh):
    placed = (P(("grp", "lat"), "lon", None), P(("lon", "lat"), None, None, None))
    return jax.shard_map(
        on_device,
        mesh=mesh,
        in_specs=placed,
        out_specs=P(("grp", "lat"), "lon", None),
        check_vma=False,
    )
```

profile of v0, /device:TPU:0, one launch (start us, length us, event | category | flops | bytes accessed | tf_op | source)
XLA Modules:
  0.0 409.2 jit_solution(5694878123159895570)
XLA Ops:
  6.5 0.0 reduce-scatter.2.cloned.1.call-start
  6.5 3.6 multiply_convert_fusion.3
  10.1 0.1 pad_maximum_fusion
  10.2 1.2 copy.24
  11.4 0.6 convert_element_type.48
  12.1 11.8 %convolution_convert_fusion = bf16[1024,24,256]{2,0,1:T(8,128)(2,1)} fusion(bf16[24,360,256]{2,1,0:T(8,128)(2,1)} %param.2, bf16[1024,360]{1,0:T(8,128)(2,1)S(1)} %convert_element_type.48), kind=kOutput, calls=%fused_computation.8 | convolution fusion | flops 4536139776 | bytes 17743872 | tf_op jit(solution)/shard_map/kn,lnc->klc/dot_general | solution.py:50
  23.9 0.0 reduce-scatter.2.cloned.1.call-update
  23.9 101.9 %reduce-scatter.2.cloned.1.call-done = bf16[256,24,256]{2,0,1:T(8,128)(2,1)} async-done(((bf16[1024,24,256]{2,0,1:T(8,128)(2,1)}), bf16[256,24,256]{2,0,1:T(8,128)(2,1)}) %reduce-scatter.2.cloned.1.call-update) | async-done | bytes 3145744 | tf_op jit(solution)/shard_map/reduce_scatter | solution.py:49
  125.8 4.0 copy.26
  129.8 4.6 %all-to-all-start = ((bf16[4,64,24,256]{3,1,2,0:T(8,128)(2,1)}), bf16[4,64,24,256]{3,1,2,0:T(8,128)(2,1)S(1)}, u32[]{:S(2)}, u32[]{:S(2)}) async-start(bf16[4,64,24,256]{3,1,2,0:T(8,128)(2,1)} %copy.26), calls=%async_computation.1 | async-start | bytes 6291456 | tf_op jit(solution)/shard_map/all_to_all | solution.py:59
  134.5 0.0 all-gather.2.cloned.1.call-start
  134.5 2.5 fusion.22
  136.9 3.8 slice_bitcast_fusion
  140.8 6.3 %maximum_bitcast_fusion = (bf16[32,1,256,512]{3,2,1,0:T(8,128)(2,1)}, bf16[32,1,256,512]{3,2,1,0:T(8,128)(2,1)}) fusion(bf16[32,256,256]{2,1,0:T(8,128)(2,1)S(1)} %get-tuple-element.5, bf16[32,256,256]{2,1,0:T(8,128)(2,1)S(1)} %get-tuple-element.6, bf16[32,256,256]{2,1,0:T(8,128)(2,1)S(1)} %fusion.22), kind=kLoop, calls=%fused_computation.6 | loop fusion | flops 33554432 | bytes 29360128 | tf_op jit(solution)/shard_map/stack | solution.py:33
  147.1 58.1 %all-to-all-done = bf16[4,64,24,256]{3,1,2,0:T(8,128)(2,1)S(1)} async-done(((bf16[4,64,24,256]{3,1,2,0:T(8,128)(2,1)}), bf16[4,64,24,256]{3,1,2,0:T(8,128)(2,1)S(1)}, u32[]{:S(2)}, u32[]{:S(2)}) %all-to-all-start) | async-done | bytes 3145760 | tf_op jit(solution)/shard_map/all_to_all | solution.py:59
  205.1 1.8 copy.39
  206.9 7.5 %bitcast_convert_fusion.1 = bf16[32,96,512]{2,1,0:T(8,128)(2,1)S(1)} fusion(bf16[32,2,96,256]{3,2,1,0:T(8,128)(2,1)S(1)} %bitcast.51, bf16[32,1,256,512]{3,2,1,0:T(8,128)(2,1)} %get-tuple-element.8, bf16[32,1,256,512]{3,2,1,0:T(8,128)(2,1)} %get-tuple-element.7), kind=kOutput, calls=%fused_computation.9 | convolution fusion | flops 1620574208 | bytes 23068672 | tf_op jit(solution)/shard_map/mplc,mpcd->mld/dot_general | solution.py:36
  214.4 0.2 copy.43
  214.7 73.6 %all_to_all.10 = bf16[4,32,24,512]{3,2,1,0:T(8,128)(2,1)} all-to-all(bf16[4,32,24,512]{3,2,1,0:T(8,128)(2,1)S(1)} %bitcast.49), channel_id=1, replica_groups=mesh['grp'=2,'lon'=4,'lat'=4] {'lat'}, dimensions={0} | all-to-all | bytes 6291456 | tf_op jit(solution)/shard_map/all_to_all | solution.py:69
  288.2 0.0 all-gather.2.cloned.1.call-update
  288.3 6.9 %multiply_convert_fusion.1 = (bf16[512,1,720]{0,2,1:T(8,128)(2,1)S(1)}, bf16[512,1,720]{0,2,1:T(8,128)(2,1)S(1)}) fusion(f32[512]{0:T(512)S(1)} %select_multiply_fusion, s32[720]{0:T(1024)S(1)} %iota_add_fusion), kind=kLoop, calls=%fused_computation.20 | loop fusion | flops 5160960 | bytes 1479488 | tf_op jit(solution)/shard_map/convert.2
  295.2 73.4 %all-gather.2.cloned.1.call-done = bf16[512,24,512]{2,1,0:T(8,128)(2,1)} async-done(((bf16[128,24,512]{2,1,0:T(8,128)(2,1)}), bf16[512,24,512]{2,1,0:T(8,128)(2,1)}) %all-gather.2.cloned.1.call-update) | async-done | bytes 12582928 | tf_op jit(solution)/shard_map/all_gather | solution.py:75
  368.7 17.1 %copy.32 = bf16[512,24,512]{0,2,1:T(8,128)(2,1)} copy(bf16[512,24,512]{2,1,0:T(8,128)(2,1)} %all-gather.2.cloned.1.call-done) | data formatting | bytes 25165824 | tf_op jit(solution)/shard_map/all_gather | solution.py:75
  385.8 16.5 %fusion.4 = bf16[24,720,256]{2,1,0:T(8,128)(2,1)} fusion(bf16[512,24,2,256]{0,3,2,1:T(8,128)(2,1)} %bitcast.47, bf16[512,1,720]{0,2,1:T(8,128)(2,1)S(1)} %get-tuple-element.10, bf16[512,1,720]{0,2,1:T(8,128)(2,1)S(1)} %get-tuple-element.9), kind=kOutput, calls=%fused_computation.5 | convolution fusion | flops 9067069440 | bytes 22904832 | tf_op jit(solution)/shard_map/mlpc,mpn->lnc/dot_general | solution.py:79
  (3 shorter events, 0.0 us)
Async XLA Ops:
  6.5 119.3 %reduce-scatter.2.cloned.1.call-start = ((), (), s32[]{:S(2)}) async-start(), calls=%async_computation.3 | async-start | bytes 15728640 | tf_op jit(solution)/shard_map/reduce_scatter | solution.py:49
  129.8 75.3 %all-to-all-start = ((bf16[4,64,24,256]{3,1,2,0:T(8,128)(2,1)}), bf16[4,64,24,256]{3,1,2,0:T(8,128)(2,1)S(1)}, u32[]{:S(2)}, u32[]{:S(2)}) async-start(bf16[4,64,24,256]{3,1,2,0:T(8,128)(2,1)} %copy.26), calls=%async_computation.1 | async-start | bytes 6291456 | tf_op jit(solution)/shard_map/all_to_all | solution.py:59
  134.5 234.2 %all-gather.2.cloned.1.call-start = ((), (), s32[]{:S(2)}) async-start(), calls=%async_computation.4 | async-start | bytes 15728640 | tf_op jit(solution)/shard_map/all_gather | solution.py:75
Sparse Core Ops, SparseCore 0:
  24.0 101.7 reduce-scatter.1
  288.4 80.2 all-gather.1
where the time goes:
time: 410 us; the launch traced here: 409 us
  waiting for transfers between devices  233 us (57%)
  blocking collectives  73.6 us (18%)
  matrix products  35.9 us (9%)
  local copies, waits for them, and re-layouts  28.9 us (7%)
  other arithmetic  19.3 us (5%)
  between operations  13.5 us (3%)
  starting transfers between devices  4.61 us (1%)
    reduce_scatter x1, waiting for transfers between devices, on_device(): lax.psum_scatter(jnp.einsum('kn,lnc->klc', table_rows, grid_field, prefer...  102 us
    all_to_all x1, blocking collectives, on_device(): lax.all_to_all(back, 'lat', 0, 0, tiled=True)  73.6 us
    all_gather x1, waiting for transfers between devices, on_device(): portion = lax.all_gather(mixed_spec, 'lon', axis=0, tiled=True)  73.4 us
    all_to_all x1, waiting for transfers between devices, on_device(): lax.all_to_all(summed.reshape(lat_count, 2 * own_modes, lat_rows, channel...  58.1 us
    all_gather x1, local copies, waits for them, and re-layouts, on_device(): portion = lax.all_gather(mixed_spec, 'lon', axis=0, tiled=True)  17.1 us
    dot_general x1, matrix products, on_device(): jnp.einsum('mlpc,mpn->lnc', parted, table_rows, preferred_element_type=jn...  16.5 us
    dot_general x1, matrix products, on_device(): jnp.einsum('kn,lnc->klc', table_rows, grid_field, preferred_element_type=...  11.8 us
    another operation x2, other arithmetic  10.5 us
  transfers between devices with their start and end apart: 3, of which 3 were waited for; matrix products, arithmetic and copies ran while one was open for 5% of the time, Pallas kernels for 0%

commit v1 on v0

--- a/solution.py
+++ b/solution.py
@@ -72,7 +72,24 @@
     out_dev = 2 * NLON // lon_count
     out_index = lon_rank * out_dev + jnp.arange(out_dev, dtype=jnp.int32)
     inv_local = synthesis_table(out_index).reshape(M, 2, out_dev)
-    portion = lax.all_gather(mixed_spec, "lon", axis=0, tiled=True)
+    size, mine, rows = (lax.axis_size("lon"), lax.axis_index("lon"), mixed_spec.shape[0])
+    forward = [(i, (i + 1) % size) for i in range(size)]
+    left = [(i, (i - 1) % size) for i in range(size)]
+    out = jnp.zeros(
+        (*mixed_spec.shape[:0], size * rows, *mixed_spec.shape[0 + 1 :]), mixed_spec.dtype
+    )
+    out = lax.dynamic_update_slice_in_dim(out, mixed_spec, mine * rows, axis=0)
+    from_left = from_right = mixed_spec
+    half = size // 2
+    for hop in range(1, half + 1):
+        from_left = lax.ppermute(from_left, "lon", forward)
+        out = lax.dynamic_update_slice_in_dim(out, from_left, (mine - hop) % size * rows, axis=0)
+        if hop < size - half:
+            from_right = lax.ppermute(from_right, "lon", left)
+            out = lax.dynamic_update_slice_in_dim(
+                out, from_right, (mine + hop) % size * rows, axis=0
+            )
+    portion = out
     count = portion.shape[0]
     table_rows = inv_local
     parted = portion.reshape(count, lat_rows, 2, channels)

time: 410 us -> 424 us (1.034)
  local copies, waits for them, and re-layouts: 28.9 us -> 44.2 us
    all_gather x1 -> x0, waiting for transfers between devices: 73.4 us -> none  [on_device(): portion = lax.all_gather(mixed_spec, 'lon', axis=0, tiled=True)]
    ppermute x0 -> x3, waiting for transfers between devices: none -> 70.3 us  [the longest x2 70.2 us: on_device(): from_left = lax.ppermute(from_left, 'lon', forward)]
    all_gather x1 -> x0, local copies, waits for them, and re-layouts: 17.1 us -> none  [on_device(): portion = lax.all_gather(mixed_spec, 'lon', axis=0, tiled=True)]
    ppermute x0 -> x3, local copies, waits for them, and re-layouts: none -> 13.9 us  [the longest x2 8.68 us: on_device(): from_left = lax.ppermute(from_left, 'lon', forward)]
    dynamic_update_slice x0 -> x4, local copies, waits for them, and re-layouts: none -> 8.2 us  [the longest x2 3.92 us: on_device(): lax.dynamic_update_slice_in_dim(out, from_left, (mine - hop) % size * row...]
    broadcast_in_dim x0 -> x1, local copies, waits for them, and re-layouts: none -> 5.88 us  [on_device(): jnp.zeros((*mixed_spec.shape[:0], size * rows, *mixed_spec.shape[0 + 1:])...]
  transfers between devices with their start and end apart: 3 -> 5, of which waited for: 3 -> 4; matrix products, arithmetic and copies ran while one was open for 5% -> 11% of each run, Pallas kernels for 0% -> 0%
where the time goes in v1:
time: 424 us
  waiting for transfers between devices  230 us (54%)
  blocking collectives  72.7 us (17%)
  local copies, waits for them, and re-layouts  44.2 us (10%)
  matrix products  36.2 us (9%)
  other arithmetic  20.3 us (5%)
  between operations  13.5 us (3%)
  starting transfers between devices  6.36 us (2%)
    reduce_scatter x1, waiting for transfers between devices, on_device(): lax.psum_scatter(jnp.einsum('kn,lnc->klc', table_rows, grid_field, prefer...  102 us
    all_to_all x1, blocking collectives, on_device(): lax.all_to_all(back, 'lat', 0, 0, tiled=True)  72.7 us
    ppermute x2, waiting for transfers between devices, on_device(): from_left = lax.ppermute(from_left, 'lon', forward)  70.2 us
    all_to_all x1, waiting for transfers between devices, on_device(): lax.all_to_all(summed.reshape(lat_count, 2 * own_modes, lat_rows, channel...  58.1 us
    dot_general x1, matrix products, on_device(): jnp.einsum('mlpc,mpn->lnc', parted, table_rows, preferred_element_type=jn...  16.9 us
    dot_general x1, matrix products, on_device(): jnp.einsum('kn,lnc->klc', table_rows, grid_field, preferred_element_type=...  11.8 us
    another operation x2, other arithmetic  11.5 us
    ppermute x2, local copies, waits for them, and re-layouts, on_device(): from_left = lax.ppermute(from_left, 'lon', forward)  8.68 us
  transfers between devices with their start and end apart: 5, of which 4 were waited for; matrix products, arithmetic and copies ran while one was open for 11% of the time, Pallas kernels for 0%

profile of v1, /device:TPU:0, one launch (start us, length us, event | category | flops | bytes accessed | tf_op | source)
XLA Modules:
  0.0 423.6 jit_solution(7855769295351368817)
XLA Ops:
  6.5 0.0 reduce-scatter.2.cloned.1.call-start
  6.5 3.6 multiply_convert_fusion.3
  10.1 0.1 pad_maximum_fusion
  10.2 1.2 copy.30
  11.4 0.6 convert_element_type.48
  12.1 11.8 %convolution_convert_fusion = bf16[1024,24,256]{2,0,1:T(8,128)(2,1)} fusion(bf16[24,360,256]{2,1,0:T(8,128)(2,1)} %param.2, bf16[1024,360]{1,0:T(8,128)(2,1)S(1)} %convert_element_type.48), kind=kOutput, calls=%fused_computation.8 | convolution fusion | flops 4536139776 | bytes 17743872 | tf_op jit(solution)/shard_map/kn,lnc->klc/dot_general | solution.py:50
  23.9 0.0 reduce-scatter.2.cloned.1.call-update
  23.9 101.9 %reduce-scatter.2.cloned.1.call-done = bf16[256,24,256]{2,0,1:T(8,128)(2,1)} async-done(((bf16[1024,24,256]{2,0,1:T(8,128)(2,1)}), bf16[256,24,256]{2,0,1:T(8,128)(2,1)}) %reduce-scatter.2.cloned.1.call-update) | async-done | bytes 3145744 | tf_op jit(solution)/shard_map/reduce_scatter | solution.py:49
  125.8 4.0 copy.32
  129.9 4.6 %all-to-all-start = ((bf16[4,64,24,256]{3,1,2,0:T(8,128)(2,1)}), bf16[4,64,24,256]{3,1,2,0:T(8,128)(2,1)S(1)}, u32[]{:S(2)}, u32[]{:S(2)}) async-start(bf16[4,64,24,256]{3,1,2,0:T(8,128)(2,1)} %copy.32), calls=%async_computation.1 | async-start | bytes 6291456 | tf_op jit(solution)/shard_map/all_to_all | solution.py:59
  134.5 2.5 fusion.22
  136.9 3.8 slice_bitcast_fusion
  140.8 6.3 %maximum_bitcast_fusion = (bf16[32,1,256,512]{3,2,1,0:T(8,128)(2,1)}, bf16[32,1,256,512]{3,2,1,0:T(8,128)(2,1)}) fusion(bf16[32,256,256]{2,1,0:T(8,128)(2,1)S(1)} %get-tuple-element.5, bf16[32,256,256]{2,1,0:T(8,128)(2,1)S(1)} %get-tuple-element.6, bf16[32,256,256]{2,1,0:T(8,128)(2,1)S(1)} %fusion.22), kind=kLoop, calls=%fused_computation.6 | loop fusion | flops 33554432 | bytes 29360128 | tf_op jit(solution)/shard_map/stack | solution.py:33
  147.1 58.1 %all-to-all-done = bf16[4,64,24,256]{3,1,2,0:T(8,128)(2,1)S(1)} async-done(((bf16[4,64,24,256]{3,1,2,0:T(8,128)(2,1)}), bf16[4,64,24,256]{3,1,2,0:T(8,128)(2,1)S(1)}, u32[]{:S(2)}, u32[]{:S(2)}) %all-to-all-start) | async-done | bytes 3145760 | tf_op jit(solution)/shard_map/all_to_all | solution.py:59
  205.1 1.8 copy.48
  206.9 7.5 %bitcast_convert_fusion.1 = bf16[32,96,512]{2,1,0:T(8,128)(2,1)S(1)} fusion(bf16[32,2,96,256]{3,2,1,0:T(8,128)(2,1)S(1)} %bitcast.53, bf16[32,1,256,512]{3,2,1,0:T(8,128)(2,1)} %get-tuple-element.8, bf16[32,1,256,512]{3,2,1,0:T(8,128)(2,1)} %get-tuple-element.7), kind=kOutput, calls=%fused_computation.9 | convolution fusion | flops 1620574208 | bytes 23068672 | tf_op jit(solution)/shard_map/mplc,mpcd->mld/dot_general | solution.py:36
  214.4 0.2 copy.52
  214.7 72.7 %all_to_all.10 = bf16[4,32,24,512]{3,2,1,0:T(8,128)(2,1)S(1)} all-to-all(bf16[4,32,24,512]{3,2,1,0:T(8,128)(2,1)S(1)} %bitcast.51), channel_id=1, replica_groups=mesh['grp'=2,'lon'=4,'lat'=4] {'lat'}, dimensions={0} | all-to-all | bytes 6291456 | tf_op jit(solution)/shard_map/all_to_all | solution.py:69
  287.4 0.0 collective-permute-start
  287.4 1.7 collective-permute-start.1
  289.2 67.9 %collective-permute-done = bf16[128,24,512]{2,1,0:T(8,128)(2,1)} collective-permute-done((bf16[128,24,512]{2,1,0:T(8,128)(2,1)S(1)}, bf16[128,24,512]{2,1,0:T(8,128)(2,1)}, u32[]{:S(2)}, u32[]{:S(2)}) %collective-permute-start) | collective-permute-done | bytes 3145760 | tf_op jit(solution)/shard_map/ppermute | solution.py:85
  357.1 0.0 collective-permute-start.2
  357.1 7.9 %multiply_convert_fusion.1 = (bf16[512,1,720]{0,2,1:T(8,128)(2,1)}, bf16[512,1,720]{0,2,1:T(8,128)(2,1)}) fusion(f32[512]{0:T(512)S(1)} %select_multiply_fusion, s32[720]{0:T(1024)S(1)} %iota_add_fusion), kind=kLoop, calls=%fused_computation.20 | loop fusion | flops 5160960 | bytes 1479488 | tf_op jit(solution)/shard_map/convert.2
  365.0 3.4 copy.38
  368.4 0.0 copy-start.2
  368.4 5.9 %broadcast_in_dim.18 = bf16[512,24,512]{0,2,1:T(8,128)(2,1)} broadcast(bf16[]{:T(256)} %constant.67.clone.1), dimensions={} | broadcast | bytes 12582914 | tf_op jit(solution)/shard_map/broadcast_in_dim | solution.py:78
  374.3 0.0 copy-done.2
  374.3 2.1 constant_dynamic-update-slice_fusion.3
  376.4 4.9 %copy.39 = bf16[128,24,512]{0,2,1:T(8,128)(2,1)} copy(bf16[128,24,512]{2,1,0:T(8,128)(2,1)} %collective-permute-done) | data formatting | bytes 6291456 | tf_op jit(solution)/shard_map/ppermute | solution.py:85
  381.4 0.0 collective-permute-done.1
  381.4 0.0 copy-start
  381.4 5.2 %copy.40 = bf16[128,24,512]{0,2,1:T(8,128)(2,1)} copy(bf16[128,24,512]{2,1,0:T(8,128)(2,1)} %collective-permute-done.1) | data formatting | bytes 6291456 | tf_op jit(solution)/shard_map/ppermute | solution.py:88
  386.6 0.0 copy-done
  386.6 0.0 copy-start.1
  386.6 1.9 constant_dynamic-update-slice_fusion.2
  388.5 1.1 copy-done.1
  389.6 2.2 constant_dynamic-update-slice_fusion.1
  391.8 2.3 collective-permute-done.2
  394.1 3.8 copy.41
  397.9 0.0 copy-start.3
  397.9 0.0 copy-start.4
  397.9 2.0 constant_dynamic-update-slice_fusion
  399.9 0.0 copy-done.3
  399.9 0.0 copy-done.4
  399.9 16.9 %fusion.4 = bf16[24,720,256]{2,1,0:T(8,128)(2,1)} fusion(bf16[512,24,2,256]{0,3,2,1:T(8,128)(2,1)} %bitcast.47, bf16[512,1,720]{0,2,1:T(8,128)(2,1)S(1)} %copy-done.4, bf16[512,1,720]{0,2,1:T(8,128)(2,1)S(1)} %copy-done.3), kind=kOutput, calls=%fused_computation.5 | convolution fusion | flops 9067069440 | bytes 22904832 | tf_op jit(solution)/shard_map/mlpc,mpn->lnc/dot_general | solution.py:96
  (3 shorter events, 0.0 us)
Async XLA Ops:
  6.5 119.3 %reduce-scatter.2.cloned.1.call-start = ((), (), s32[]{:S(2)}) async-start(), calls=%async_computation.3 | async-start | bytes 15728640 | tf_op jit(solution)/shard_map/reduce_scatter | solution.py:49
  129.9 75.3 %all-to-all-start = ((bf16[4,64,24,256]{3,1,2,0:T(8,128)(2,1)}), bf16[4,64,24,256]{3,1,2,0:T(8,128)(2,1)S(1)}, u32[]{:S(2)}, u32[]{:S(2)}) async-start(bf16[4,64,24,256]{3,1,2,0:T(8,128)(2,1)} %copy.32), calls=%async_computation.1 | async-start | bytes 6291456 | tf_op jit(solution)/shard_map/all_to_all | solution.py:59
  287.4 69.7 %collective-permute-start = (bf16[128,24,512]{2,1,0:T(8,128)(2,1)S(1)}, bf16[128,24,512]{2,1,0:T(8,128)(2,1)}, u32[]{:S(2)}, u32[]{:S(2)}) collective-permute-start(bf16[128,24,512]{2,1,0:T(8,128)(2,1)S(1)} %bitcast.48), channel_id=1, source_target_pairs={{0,4},{4,8},{8,12},{12,0},{1,5},{5,9},{9,13},{13,1},{2,6},{6,10},{... | collective-permute-start | bytes 9437192 | tf_op jit(solution)/shard_map/ppermute | solution.py:85
  287.4 93.9 %collective-permute-start.1 = (bf16[128,24,512]{2,1,0:T(8,128)(2,1)S(1)}, bf16[128,24,512]{2,1,0:T(8,128)(2,1)}, u32[]{:S(2)}, u32[]{:S(2)}) collective-permute-start(bf16[128,24,512]{2,1,0:T(8,128)(2,1)S(1)} %bitcast.49), channel_id=1, source_target_pairs={{0,12},{4,0},{8,4},{12,8},{1,13},{5,1},{9,5},{13,9},{2,14},{6,2},{... | collective-permute-start | bytes 9437192 | tf_op jit(solution)/shard_map/ppermute | solution.py:88
  357.1 37.0 %collective-permute-start.2 = (bf16[128,24,512]{2,1,0:T(8,128)(2,1)}, bf16[128,24,512]{2,1,0:T(8,128)(2,1)}, u32[]{:S(2)}, u32[]{:S(2)}) collective-permute-start(bf16[128,24,512]{2,1,0:T(8,128)(2,1)} %collective-permute-done), channel_id=1, source_target_pairs={{0,4},{4,8},{8,12},{12,0},{1,5},{5,9},{9,13},{13,1},{2,6},{6,10},{... | collective-permute-start | bytes 9437192 | tf_op jit(solution)/shard_map/ppermute | solution.py:85
  368.4 5.9 %copy-start.2 = (bf16[128,24,512]{0,2,1:T(8,128)(2,1)S(1)}, bf16[128,24,512]{0,2,1:T(8,128)(2,1)}, u32[]{:S(2)}) copy-start(bf16[128,24,512]{0,2,1:T(8,128)(2,1)} %copy.38) | copy-start | bytes 9437188
  381.4 5.2 %copy-start = (bf16[128,24,512]{0,2,1:T(8,128)(2,1)S(1)}, bf16[128,24,512]{0,2,1:T(8,128)(2,1)}, u32[]{:S(2)}) copy-start(bf16[128,24,512]{0,2,1:T(8,128)(2,1)} %copy.39) | copy-start | bytes 9437188
  386.6 3.0 copy-start.1
  397.9 2.0 copy-start.3
  397.9 2.0 copy-start.4
Sparse Core Ops, SparseCore 0:
  24.1 101.7 reduce-scatter.1
